TPU v7x, 1024 devices: a whole 4x8x16 slice. The times are simulated.
1024 devices in a mesh: expert: 32 (over z, core), col: 8 (over y), dp: 4 (over x).
Axes of the slice: x: 4, y: 8, z: 16, core: 2. Of those that a mesh axis runs over, the one named last changes fastest.
Arguments:
- tokens: bfloat16 [16384, 8192], P(('expert', 'dp'), 'col'), may hold values from -6 to 6
- cotangent: bfloat16 [16384, 8192], P(('expert', 'dp'), 'col'), may hold values from -6 to 6
- expert_ids: int32 [16384, 4], P(('expert', 'dp')), may hold values from 0 to 63, all different within a row; in each aligned block of 128 rows (0 to 127, 128 to 255, ...) at most 10 rows name the same one
- gate_codes: int32 [16384, 4], P(('expert', 'dp')), may hold values from 1 to 255
- w_in: bfloat16 [64, 8192, 448], P('expert', 'col'), may hold values from -0.0625 to 0.0625
- w_out: bfloat16 [64, 224, 8192], P('expert', None, 'col'), may hold values from -0.375 to 0.375
Outputs:
- grad_tokens: bfloat16 [16384, 8192], P(('expert', 'dp'), 'col')
- grad_in: float32 [64, 8192, 448], P('expert', ('col', 'dp'))
Inputs may be any that keep to these rules, and one draw needn't show every extreme that they name: `expert_ids`: each token names 4 different experts. In each aligned block of 128 tokens (the tokens of one device) no expert is named by more than 10 tokens, a bound that some block reaches; every expert is named somewhere.
All inputs are finite; a program needn't handle non-finite values.
Results may differ from a plain program's by a relative error of at most 0.0064.
Values may be sent and summed in bfloat16 or wider, within the bound.
A program may use at most 32 MiB of HBM per device.

v0:
```python
import jax
import jax.numpy as jnp
from jax import lax
from jax.sharding import PartitionSpec as P


def activate_grad(gate_up, hidden_grad, hidden_dim):
    gate_half = gate_up[..., :hidden_dim]
    up_half = gate_up[..., hidden_dim:]
    sigmoid_gate = jax.nn.sigmoid(gate_half)
    grad_gate = hidden_grad * up_half * sigmoid_gate * (1.0 + gate_half * (1.0 - sigmoid_gate))
    grad_up = hidden_grad * gate_half * sigmoid_gate
    return jnp.concatenate([grad_gate, grad_up], axis=-1).astype(jnp.bfloat16)


def send_rows(block):
    return lax.all_to_all(block, "expert", split_axis=0, concat_axis=1, tiled=True)


def route_places(flat_ids, experts):
    route_count = flat_ids.shape[0]
    width = 128
    blocks = route_count // width
    ids_block = flat_ids.reshape(blocks, width)
    earlier = (
        jnp.arange(width, dtype=jnp.int32)[None, :] < jnp.arange(width, dtype=jnp.int32)[:, None]
    )
    same = (ids_block[:, :, None] == ids_block[:, None, :]) & earlier[None, :, :]
    within = jnp.sum(same.astype(jnp.int32), axis=2)
    onehot = (ids_block[:, :, None] == jnp.arange(experts, dtype=jnp.int32)[None, None, :]).astype(
        jnp.int32
    )
    counts = jnp.sum(onehot, axis=1)
    before = jnp.cumsum(counts, axis=0) - counts
    offset = jnp.sum(onehot * before[:, None, :], axis=2)
    return (within + offset).reshape(route_count)


def per_device(tokens, cotangent, expert_ids, gate_codes, w_in, w_out):
    token_count, feature_dim = tokens.shape
    top_k = expert_ids.shape[1]
    owners = lax.axis_size("expert")
    local_experts = w_in.shape[0]
    hidden_dim = w_out.shape[1]
    experts = local_experts * owners
    route_count = token_count * top_k
    capacity = route_count // experts * 5 // 4
    flat_ids = expert_ids.reshape(route_count)
    position = route_places(flat_ids, experts)
    slot_index = flat_ids * capacity + position
    route_of_slot = jnp.full((experts * capacity,), route_count, jnp.int32)
    route_of_slot = route_of_slot.at[slot_index].set(jnp.arange(route_count, dtype=jnp.int32))
    live_slot = route_of_slot < route_count
    bounded = jnp.minimum(route_of_slot, route_count - 1)
    token_of_slot = bounded // top_k
    gate_values = gate_codes.astype(jnp.float32)
    route_weight = (gate_values / jnp.sum(gate_values, axis=1, keepdims=True)).reshape(route_count)
    slot_weight = jnp.where(live_slot, route_weight[bounded], 0.0)
    rows_send = jnp.where(live_slot[:, None], tokens[token_of_slot], jnp.zeros((), jnp.bfloat16))
    grads_send = (slot_weight[:, None] * cotangent[token_of_slot].astype(jnp.float32)).astype(
        jnp.bfloat16
    )
    rows_in = send_rows(rows_send.reshape(experts, capacity, feature_dim))
    rows_grad = send_rows(grads_send.reshape(experts, capacity, feature_dim))
    gate_part = jnp.einsum("erd,edf->erf", rows_in, w_in, preferred_element_type=jnp.float32)
    hidden_part = jnp.einsum("erd,efd->erf", rows_grad, w_out, preferred_element_type=jnp.float32)
    gate_up, hidden_grad = lax.psum((gate_part, hidden_part), "col")
    grad_gate_up = activate_grad(gate_up, hidden_grad, hidden_dim)
    route_grad = jnp.einsum(
        "erf,edf->erd", grad_gate_up, w_in, preferred_element_type=jnp.float32
    ).astype(jnp.bfloat16)
    returned = lax.all_to_all(route_grad, "expert", split_axis=1, concat_axis=0, tiled=True)
    per_route = returned.reshape(experts * capacity, feature_dim)[slot_index]
    grad_tokens = jnp.sum(
        per_route.reshape(token_count, top_k, feature_dim).astype(jnp.float32), axis=1
    ).astype(jnp.bfloat16)
    partial_grad = jnp.einsum(
        "erd,erf->edf", rows_in, grad_gate_up, preferred_element_type=jnp.float32
    )
    grad_in = lax.psum_scatter(partial_grad, "dp", scatter_dimension=1, tiled=True)
    return (grad_tokens, grad_in)


def solution(mesh):
    placed = (
        P(("expert", "dp"), "col"),
        P(("expert", "dp"), "col"),
        P(("expert", "dp"), None),
        P(("expert", "dp"), None),
        P("expert", "col", None),
        P("expert", None, "col"),
    )
    return jax.shard_map(
        per_device,
        mesh=mesh,
        in_specs=placed,
        out_specs=(P(("expert", "dp"), "col"), P("expert", ("col", "dp"), None)),
        check_vma=False,
    )
```

profile of v0, /device:TPU:6, one launch (start us, length us, event | category | flops | bytes accessed | tf_op | source)
XLA Modules:
  0.0 453.9 jit_solution(15470707241782087694)
XLA Ops:
  7.2 0.0 copy-start
  7.2 0.8 broadcast_multiply_fusion
  8.0 0.8 copy.34
  8.8 0.1 copy.33
  8.9 0.1 mul.55
  9.0 0.1 eq.28
  9.2 0.1 convert_reduce_fusion.1
  9.3 0.2 convert_reduce_fusion
  9.6 0.1 select_reduce_fusion
  9.8 2.4 scatter_custom_fusion
  12.3 2.8 gather_fusion.1
  15.1 0.0 copy-start.6
  15.1 2.1 reshape.105
  17.3 0.1 copy.35
  17.4 0.1 reshape.102
  17.5 4.3 gather_fusion
  21.8 0.1 mul.58
  22.0 3.8 multiply_convert_fusion
  25.8 19.4 %all-to-all-start = ((bf16[64,10,1024]{2,1,0:T(8,128)(2,1)}), bf16[64,10,1024]{2,1,0:T(8,128)(2,1)}, u32[]{:S(2)}, u32[]{:S(2)}) async-start(bf16[64,10,1024]{2,1,0:T(8,128)(2,1)} %multiply_convert_fusion), calls=%async_computation | async-start | bytes 4194304 | tf_op jit(solution)/shard_map/all_to_all | solution.py:17
  45.2 2.8 gather_fusion.2
  48.0 1.5 gather.17
  49.6 0.1 broadcast_in_dim.38
  49.7 3.1 broadcast_select_fusion
  52.9 91.5 %all-to-all-done = bf16[64,10,1024]{2,1,0:T(8,128)(2,1)} async-done(((bf16[64,10,1024]{2,1,0:T(8,128)(2,1)}), bf16[64,10,1024]{2,1,0:T(8,128)(2,1)}, u32[]{:S(2)}, u32[]{:S(2)}) %all-to-all-start) | async-done | bytes 1310752 | tf_op jit(solution)/shard_map/all_to_all | solution.py:17
  144.4 4.8 %all-to-all-start.1 = ((bf16[64,10,1024]{2,1,0:T(8,128)(2,1)}), bf16[64,10,1024]{2,1,0:T(8,128)(2,1)}, u32[]{:S(2)}, u32[]{:S(2)}) async-start(bf16[64,10,1024]{2,1,0:T(8,128)(2,1)} %broadcast_select_fusion), calls=%async_computation.1 | async-start | bytes 4194304 | tf_op jit(solution)/shard_map/all_to_all | solution.py:17
  149.2 0.0 all-reduce.3.cloned.1.call-start
  149.2 4.0 copy.46
  153.3 97.3 %all-to-all-done.1 = bf16[64,10,1024]{2,1,0:T(8,128)(2,1)} async-done(((bf16[64,10,1024]{2,1,0:T(8,128)(2,1)}), bf16[64,10,1024]{2,1,0:T(8,128)(2,1)}, u32[]{:S(2)}, u32[]{:S(2)}) %all-to-all-start.1) | async-done | bytes 1310752 | tf_op jit(solution)/shard_map/all_to_all | solution.py:17
  250.6 3.1 copy.48
  253.7 1.4 fusion
  255.1 2.0 fusion.4
  257.1 0.0 all-reduce.3.cloned.1.call-update
  257.1 0.2 reduce-scatter.2.cloned.1.call-start
  257.3 88.4 %all-reduce.3.cloned.1.call-done = (f32[2,320,224]{2,1,0:T(8,128)}, f32[2,320,448]{2,1,0:T(8,128)}) async-done(((f32[2,320,224]{2,1,0:T(8,128)}, f32[2,320,448]{2,1,0:T(8,128)}), (f32[2,320,224]{2,1,0:T(8,128)}, f32[2,320,448]{2,1,0:T(8,128)})) %all-reduce.3.cloned.1.call-update) | async-done | bytes 1720336 | tf_op jit(solution)/shard_map/psum | solution.py:67
  345.7 1.9 fusion.8
  347.6 0.7 copy-done.3
  348.3 3.1 fusion.2
  351.5 0.0 reduce-scatter.2.cloned.1.call-update
  351.5 0.9 copy-done.4
  352.5 0.9 convolution_convert_fusion
  353.4 2.4 copy.42
  355.8 13.3 %all-to-all-start.2 = ((bf16[2,320,1024]{2,0,1:T(2,128)(2,1)}), bf16[2,320,1024]{2,0,1:T(2,128)(2,1)S(1)}, u32[]{:S(2)}, u32[]{:S(2)}) async-start(bf16[2,320,1024]{2,0,1:T(2,128)(2,1)} %copy.42), calls=%async_computation.2 | async-start | bytes 2621440 | tf_op jit(solution)/shard_map/all_to_all | solution.py:72
  369.1 67.1 %all-to-all-done.2 = bf16[2,320,1024]{2,0,1:T(2,128)(2,1)S(1)} async-done(((bf16[2,320,1024]{2,0,1:T(2,128)(2,1)}), bf16[2,320,1024]{2,0,1:T(2,128)(2,1)S(1)}, u32[]{:S(2)}, u32[]{:S(2)}) %all-to-all-start.2) | async-done | bytes 1310752 | tf_op jit(solution)/shard_map/all_to_all | solution.py:72
  436.2 1.9 copy.43
  438.1 2.6 reshape.103
  440.7 2.8 gather_fusion.3
  443.4 1.5 reshape.104
  444.9 2.1 reduce_sum.52
  (25 shorter events, 0.2 us)
Async XLA Ops:
  7.2 247.9 %copy-start = (bf16[2,1024,448]{1,2,0:T(8,128)(2,1)S(1)}, bf16[2,1024,448]{1,2,0:T(8,128)(2,1)}, u32[]{:S(2)}) copy-start(bf16[2,1024,448]{1,2,0:T(8,128)(2,1)} %param.10) | copy-start | bytes 5505028
  7.2 5.1 %copy-start.1 = (bf16[128,1024]{1,0:T(8,128)(2,1)S(1)}, bf16[128,1024]{1,0:T(8,128)(2,1)}, u32[]{:S(2)}) copy-start(bf16[128,1024]{1,0:T(8,128)(2,1)} %param.7) | copy-start | bytes 786436
  15.1 2.1 copy-start.6
  25.8 19.4 %copy-start.2 = (bf16[128,1024]{1,0:T(8,128)(2,1)S(1)}, bf16[128,1024]{1,0:T(8,128)(2,1)}, u32[]{:S(2)}) copy-start(bf16[128,1024]{1,0:T(8,128)(2,1)} %param.6) | copy-start | bytes 786436
  25.8 118.6 %all-to-all-start = ((bf16[64,10,1024]{2,1,0:T(8,128)(2,1)}), bf16[64,10,1024]{2,1,0:T(8,128)(2,1)}, u32[]{:S(2)}, u32[]{:S(2)}) async-start(bf16[64,10,1024]{2,1,0:T(8,128)(2,1)} %multiply_convert_fusion), calls=%async_computation | async-start | bytes 4194304 | tf_op jit(solution)/shard_map/all_to_all | solution.py:17
  144.4 106.2 %all-to-all-start.1 = ((bf16[64,10,1024]{2,1,0:T(8,128)(2,1)}), bf16[64,10,1024]{2,1,0:T(8,128)(2,1)}, u32[]{:S(2)}, u32[]{:S(2)}) async-start(bf16[64,10,1024]{2,1,0:T(8,128)(2,1)} %broadcast_select_fusion), calls=%async_computation.1 | async-start | bytes 4194304 | tf_op jit(solution)/shard_map/all_to_all | solution.py:17
  149.2 196.5 %all-reduce.3.cloned.1.call-start = ((), (), s32[]{:S(2)}) async-start(), calls=%async_computation.5 | async-start | bytes 3932160 | tf_op jit(solution)/shard_map/psum | solution.py:67
  250.6 3.1 copy-start.5
  250.6 3.1 copy-start.7
  257.1 189.9 %reduce-scatter.2.cloned.1.call-start = ((), (), s32[]{:S(2)}) async-start(), calls=%async_computation.4 | async-start | bytes 4587520 | tf_op jit(solution)/shard_map/reduce_scatter | solution.py:80
  347.6 0.7 copy-start.3
  351.5 1.0 copy-start.4
  355.8 80.4 %all-to-all-start.2 = ((bf16[2,320,1024]{2,0,1:T(2,128)(2,1)}), bf16[2,320,1024]{2,0,1:T(2,128)(2,1)S(1)}, u32[]{:S(2)}, u32[]{:S(2)}) async-start(bf16[2,320,1024]{2,0,1:T(2,128)(2,1)} %copy.42), calls=%async_computation.2 | async-start | bytes 2621440 | tf_op jit(solution)/shard_map/all_to_all | solution.py:72
Sparse Core Ops, SparseCore 0:
  257.2 88.4 all-reduce.2
  351.6 50.4 reduce-scatter.1
where the time goes:
time: 456 us; the launch traced here: 454 us
  waiting for transfers between devices  344 us (75%)
  starting transfers between devices  37.7 us (8%)
  local copies, waits for them, and re-layouts  37.6 us (8%)
  between operations  14.3 us (3%)
  other arithmetic  12.4 us (3%)
  matrix products  7.39 us (2%)
    all_to_all x2, waiting for transfers between devices, send_rows(): lax.all_to_all(block, 'expert', split_axis=0, concat_axis=1, tiled=True)  189 us
    psum x1, waiting for transfers between devices, per_device(): gate_up, hidden_grad = lax.psum((gate_part, hidden_part), 'col')  88.4 us
    all_to_all x1, waiting for transfers between devices, per_device(): lax.all_to_all(route_grad, 'expert', split_axis=1, concat_axis=0, tiled=T...  67.1 us
    all_to_all x2, starting transfers between devices, send_rows(): lax.all_to_all(block, 'expert', split_axis=0, concat_axis=1, tiled=True)  24.2 us
    all_to_all x1, starting transfers between devices, per_device(): lax.all_to_all(route_grad, 'expert', split_axis=1, concat_axis=0, tiled=T...  13.3 us
  transfers between devices with their start and end apart: 5, of which 4 were waited for; matrix products, arithmetic and copies ran while one was open for 6% of the time, Pallas kernels for 0%

commit v1 on v0

v1 whole, which is shorter than its diff:
```python
import functools

import jax
import jax.numpy as jnp
from jax import lax
from jax.experimental import pallas as pl
from jax.experimental.pallas import tpu as pltpu
from jax.sharding import PartitionSpec as P

MESH = pl.DeviceIdType.MESH
BF16, F32 = jnp.bfloat16, jnp.float32
TILE = 256


def dot(a, b):
    return jnp.dot(a, b, preferred_element_type=F32)


def dot_nt(a, b):
    return lax.dot_general(a, b, (((1,), (1,)), ((), ())), preferred_element_type=F32)


def dot_tn(a, b):
    return lax.dot_general(a, b, (((0,), (0,)), ((), ())), preferred_element_type=F32)


def kernel(
    cap, ring, cols, groups, stagger,
    ids_ref, codes_ref, tok_ref, cot_ref, win_ref, wout_ref,
    gtok_ref, gin_ref,
    aux, land_t, land_c, win4, wout4, pick, pick_t, slot_w, xt, xc,
    part_gu, part_h, recv_gu, recv_h, gg, rg, contrib, first, rs_r, rs_l,
    peer_x, peer_g, dp_out, dp_in,
    s_loc, s_peer, r_peer, s_aux, r_aux, s_ag, r_ag, s_gu, r_gu, s_h, r_h, s_gg, r_gg, s_rs, r_rs, s_dp, r_dp, go,
):
    T, D = tok_ref.shape
    F = wout_ref.shape[1]
    half = ring // 2
    NB = half
    UR = cap * NB
    R2 = 4 * UR
    R = 2 * R2
    QR = R // cols
    CH = 2
    TC = T // CH
    tile = min(TILE, D)
    me = lax.axis_index("expert")
    z, core = me // 2, me % 2
    my_q = lax.axis_index("col")
    my_g = lax.axis_index("dp")
    right = {"expert": lax.rem(me + 2, 2 * ring)}
    left = {"expert": lax.rem(me + 2 * ring - 2, 2 * ring)}
    mate = {"expert": me + 1 - 2 * core}
    cols_at = [{"col": lax.rem(my_q + d, cols)} for d in range(cols)]
    groups_at = [{"dp": lax.rem(my_g + d, groups)} for d in range(groups)]
    ways = (right, left)

    partners = [right, left, mate] + cols_at[1:] + groups_at[1:]
    barrier = pltpu.get_barrier_semaphore()
    for other in partners:
        pl.semaphore_signal(barrier, inc=1, device_id=other, device_id_type=MESH)
    pl.semaphore_wait(barrier, len(partners))

    sent = []

    def push(src, dst, send_sem, recv_sem, where):
        copy = pltpu.make_async_remote_copy(
            src_ref=src, dst_ref=dst, send_sem=send_sem, recv_sem=recv_sem, device_id=where, device_id_type=MESH
        )
        copy.start()
        sent.append(copy)
        return copy

    mine = pl.ds(2 * core, 2)
    local = [
        pltpu.make_async_copy(win_ref, win4.at[mine], s_loc.at[0]),
        pltpu.make_async_copy(wout_ref, wout4.at[mine], s_loc.at[1]),
    ]
    for copy in local:
        copy.start()
    w_in_copy = push(win_ref, win4.at[mine], s_peer.at[0], r_peer.at[0], mate)
    w_out_copy = push(wout_ref, wout4.at[mine], s_peer.at[1], r_peer.at[1], mate)

    codes = codes_ref[...].astype(F32)
    aux[0, 0:4, :] = ids_ref[...].astype(F32)
    aux[0, 4:8, :] = codes / jnp.sum(codes, axis=0, keepdims=True)
    land_t[0:T, :] = tok_ref[...]
    land_c[0:T, :] = cot_ref[...]

    if stagger:
        @pl.when(core == 1)
        def _():
            pl.semaphore_wait(go, 1)

    def place(way, k):
        if k == 0:
            return 0
        if k == half:
            return 2 * half - 1
        return 2 * k if way == 0 else 2 * k - 1

    land = (land_t, land_c)
    ag = {}
    aux_copy = {}

    def carries(way, k, c):
        return k < half or c == way

    def pass_on(arr, way, k, c):
        if k > half or not carries(way, k, c):
            return
        src = land[arr].at[pl.ds(place(way, k - 1) * T + c * TC, TC)]
        dst = land[arr].at[pl.ds(place(way, k) * T + c * TC, TC)]
        ag[arr, way, k, c] = push(src, dst, s_ag.at[arr, way, k - 1, c], r_ag.at[arr, way, k - 1, c], ways[way])

    def pass_aux(way, k):
        if k < half or (k == half and way == 0):
            aux_copy[way, k] = push(
                aux.at[place(way, k - 1)], aux.at[place(way, k)],
                s_aux.at[way, k - 1], r_aux.at[way, k - 1], ways[way],
            )

    def arrived(arr, k):
        for c in range(CH):
            for way in range(2):
                if (arr, way, k, c) in ag:
                    ag[arr, way, k, c].wait_recv()
                    pass_on(arr, way, k + 1, c)
        if arr == 0:
            for way in range(2):
                if (way, k) in aux_copy:
                    aux_copy[way, k].wait_recv()
                    pass_aux(way, k + 1)

    before = (lax.broadcasted_iota(jnp.int32, (T, T), 0) < lax.broadcasted_iota(jnp.int32, (T, T), 1)).astype(F32).astype(BF16)
    block_of = lax.broadcasted_iota(jnp.int32, (NB, T), 0)

    def build_pick(h):
        info = aux[h * NB:(h + 1) * NB]
        ids = [info[:, k, :] for k in range(4)]
        weights = [info[:, 4 + k, :] for k in range(4)]
        member, weight = [], []
        for e in range(4):
            number = (4 * z + e).astype(F32)
            hits = [ids[k] == number for k in range(4)]
            member.append(sum(jnp.where(hit, 1.0, 0.0) for hit in hits))
            weight.append(sum(jnp.where(hits[k], weights[k], 0.0) for k in range(4)))
        order = dot(jnp.concatenate(member, axis=0).astype(BF16), before)
        chosen, rows_w = [], []
        for e in range(4):
            at = order[e * NB:(e + 1) * NB]
            for j in range(cap):
                one = jnp.where(at == float(j), member[e], 0.0)
                chosen.append(one)
                rows_w.append(jnp.sum(one * weight[e], axis=1, keepdims=True))
        slot_w[h] = jnp.broadcast_to(jnp.concatenate(rows_w, axis=0), (R2, 128))
        for i in range(NB):
            rows = jnp.concatenate([jnp.where(block_of == i, one, 0.0) for one in chosen], axis=0)
            pick[h, :, i * T:(i + 1) * T] = rows.astype(BF16)
            pick_t[h * NB + i] = rows.T.astype(BF16)

    def compact(arr, h):
        def body(n, carry):
            at = pl.ds(pl.multiple_of(n * tile, tile), tile)
            rows = dot(pick[h], land[arr][h * NB * T:(h + 1) * NB * T, at])
            if arr == 1:
                rows = rows * slot_w[h][:, 0:1]
            rows = rows.astype(BF16)
            for e in range(4):
                (xt, xc)[arr][e, h * UR:(h + 1) * UR, at] = rows[e * UR:(e + 1) * UR]
            return carry
        lax.fori_loop(0, D // tile, body, 0)

    def gate_up(e, carry):
        rows = pl.ds(pl.multiple_of(e * 2 * UR, 2 * UR), 2 * UR)
        part_gu[0, rows, :] = dot_nt(xt[e], win4[e, 0:F, :])
        part_gu[1, rows, :] = dot_nt(xt[e], win4[e, F:2 * F, :])
        return carry

    def hidden(e, carry):
        rows = pl.ds(pl.multiple_of(e * 2 * UR, 2 * UR), 2 * UR)
        part_h[rows, :] = dot_nt(xc[e], wout4[e])
        return carry

    def rows_of(d):
        return pl.ds(pl.multiple_of(lax.rem(my_q + d, cols) * QR, QR), QR)

    far_first = sorted(range(1, cols), key=lambda d: -min(d, cols - d))
    gu_copies, h_copies, gg_copies, peer_copies = [], [], [], []

    def send_gate_up():
        for copy in local:
            copy.wait()
        w_in_copy.wait_recv()
        w_out_copy.wait_recv()
        lax.fori_loop(0, 4, gate_up, 0)
        for d in far_first:
            gu_copies.append(push(part_gu.at[:, rows_of(d)], recv_gu.at[d - 1], s_gu.at[d - 1], r_gu.at[d - 1], cols_at[d]))
        peer_copies.append(push(xt.at[pl.ds(2 - 2 * core, 2)], peer_x, s_peer.at[2], r_peer.at[2], mate))

    tasks = [
        (0, half // 2, lambda: build_pick(0)),
        (0, half // 2 + 1, lambda: compact(0, 0)),
        (1, 1, lambda: build_pick(1)),
        (1, 2, lambda: compact(0, 1)),
        (1, 3, send_gate_up),
        (1, half // 2 + 1, lambda: compact(1, 0)),
    ]

    def work(arr, k):
        if tasks and (tasks[0][0], tasks[0][1]) <= (arr, k):
            tasks.pop(0)[2]()

    for way in range(2):
        pass_aux(way, 1)
    for arr in range(2):
        for c in range(CH):
            for way in range(2):
                pass_on(arr, way, 1, c)
        if arr == 1:
            arrived(0, half)
        for k in range(1, half):
            arrived(arr, k)
            work(arr, k)
    while tasks:
        work(2, 0)
    arrived(1, half)
    if stagger:
        pl.semaphore_signal(go, inc=1, device_id=mate, device_id_type=MESH)
    compact(1, 1)
    lax.fori_loop(0, 4, hidden, 0)
    for d in far_first:
        h_copies.append(push(part_h.at[rows_of(d)], recv_h.at[d - 1], s_h.at[d - 1], r_h.at[d - 1], cols_at[d]))

    own = rows_of(0)
    gate, up = part_gu[0, own, :], part_gu[1, own, :]
    for copy in gu_copies:
        copy.wait_recv()
    for d in range(cols - 1):
        gate = gate + recv_gu[d, 0]
        up = up + recv_gu[d, 1]
    s = jax.nn.sigmoid(gate)
    slope = up * s * (1.0 + gate * (1.0 - s))
    act = gate * s
    grad = part_h[own, :]
    for copy in h_copies:
        copy.wait_recv()
    for d in range(cols - 1):
        grad = grad + recv_h[d]
    gg[0, own, :] = (grad * slope).astype(BF16)
    gg[1, own, :] = (grad * act).astype(BF16)
    for d in far_first:
        gg_copies.append(push(gg.at[:, own], gg.at[:, own], s_gg.at[d - 1], r_gg.at[d - 1], cols_at[d]))
    for d in range(1, cols):
        pltpu.make_async_remote_copy(
            src_ref=gg.at[:, rows_of(cols - d)], dst_ref=gg.at[:, rows_of(cols - d)], send_sem=s_gg.at[d - 1],
            recv_sem=r_gg.at[d - 1], device_id=cols_at[d], device_id_type=MESH,
        ).wait_recv()
    theirs = pl.ds(pl.multiple_of((1 - core) * R2, R2), R2)
    peer_copies.append(push(gg.at[:, theirs], peer_g, s_peer.at[3], r_peer.at[3], mate))

    def route_grad(e, carry):
        rows = pl.ds(pl.multiple_of(e * 2 * UR, 2 * UR), 2 * UR)
        g0, g1 = gg[0, rows, :], gg[1, rows, :]
        at = pl.ds(pl.multiple_of(e * UR, UR), UR)

        def body(n, carry):
            lanes = pl.ds(pl.multiple_of(n * tile, tile), tile)
            both = (dot(g0, win4[e, 0:F, lanes]) + dot(g1, win4[e, F:2 * F, lanes])).astype(BF16)
            rg[0, at, lanes] = both[0:UR]
            rg[1, at, lanes] = both[UR:2 * UR]
            return carry
        return lax.fori_loop(0, D // tile, body, carry)

    lax.fori_loop(0, 4, route_grad, 0)

    def contribution(into, p):
        def body(n, carry):
            lanes = pl.ds(pl.multiple_of(n * tile, tile), tile)
            contrib[into, :, lanes] = dot(pick_t[p], rg[p // NB, :, lanes])
            return carry
        lax.fori_loop(0, D // tile, body, 0)

    share = D // groups

    def weight_grad(d):
        lanes = pl.ds(pl.multiple_of(lax.rem(my_g + d, groups) * share, share), share)
        for l in range(2):
            rows = pl.ds(pl.multiple_of((2 * core + l) * 2 * UR, 2 * UR), 2 * UR)
            x = jnp.concatenate([xt[2 * core + l, :, lanes], peer_x[l, :, lanes]], axis=0)
            for g in range(2):
                grads = jnp.concatenate([gg[g, rows, :], peer_g[g, l * 2 * UR:(l + 1) * 2 * UR, :]], axis=0)
                value = dot_tn(grads, x)
                if d == 0:
                    gin_ref[l, g * F:(g + 1) * F, :] = value
                else:
                    dp_out[d - 1, l, g * F:(g + 1) * F, :] = value.astype(BF16)

    dp_copies = []

    def send_weight_grad(d):
        weight_grad(d)
        dp_copies.append(push(dp_out.at[d - 1], dp_in.at[d - 1], s_dp.at[d - 1], r_dp.at[d - 1], groups_at[d]))

    def peers_ready():
        for copy in peer_copies:
            copy.wait_recv()

    later = [peers_ready]
    for d in sorted(range(1, groups), key=lambda d: -min(d, groups - d)):
        later.append(functools.partial(send_weight_grad, d))
    later.append(lambda: weight_grad(0))

    if stagger:
        @pl.when(core == 0)
        def _():
            pl.semaphore_wait(go, 1)
    rs = (rs_r, rs_l)
    rs_copy = {}

    def rs_send(way, k, c, src):
        rs_copy[way, k, c] = push(
            src, rs[way].at[k - 1, pl.ds(c * TC, TC)], s_rs.at[way, k - 1, c], r_rs.at[way, k - 1, c], ways[way]
        )

    contribution(0, 2 * half - 1)
    for way in range(2):
        first[way] = contrib[0, way * TC:(way + 1) * TC, :].astype(BF16)
        rs_send(way, 1, way, first.at[way])
    for k in range(2, half + 1):
        o = half + 1 - k
        for way in range(2):
            contribution(way, 2 * o - 1 + way)
        for c in range(CH):
            for way in range(2):
                at = pl.ds(c * TC, TC)
                total = contrib[way, c * TC:(c + 1) * TC, :]
                if (way, k - 1, c) in rs_copy:
                    rs_copy[way, k - 1, c].wait_recv()
                    total = total + rs[way][k - 2, c * TC:(c + 1) * TC, :].astype(F32)
                rs[way][k - 2, c * TC:(c + 1) * TC, :] = total.astype(BF16)
                rs_send(way, k, c, rs[way].at[k - 2, at])
        if later:
            later.pop(0)()
    while later:
        later.pop(0)()
    contribution(0, 0)
    for c in range(CH):
        at = slice(c * TC, (c + 1) * TC)
        total = contrib[0, at, :]
        for way in range(2):
            rs_copy[way, half, c].wait_recv()
            total = total + rs[way][half - 1, at, :].astype(F32)
        gtok_ref[at, :] = total.astype(BF16)
    for copy in dp_copies:
        copy.wait_recv()
    for l in range(2):
        total = gin_ref[l]
        for d in range(groups - 1):
            total = total + dp_in[d, l].astype(F32)
        gin_ref[l] = total
    for copy in sent:
        copy.wait_send()


def per_device(stagger, tokens, cotangent, expert_ids, gate_codes, w_in, w_out):
    T, D = tokens.shape
    top = expert_ids.shape[1]
    F = w_out.shape[1]
    owners, cols, groups = lax.axis_size("expert"), lax.axis_size("col"), lax.axis_size("dp")
    ring = owners // 2
    half = ring // 2
    experts = w_in.shape[0] * owners
    cap = T * top // experts * 5 // 4
    UR = cap * half
    R2, R = 4 * UR, 8 * UR
    QR = R // cols
    share = D // groups
    V = pltpu.VMEM
    DMA = pltpu.SemaphoreType.DMA
    scratch = [
        V((ring, 8, T), F32),
        V((ring * T, D), BF16), V((ring * T, D), BF16),
        V((4, 2 * F, D), BF16), V((4, F, D), BF16),
        V((2, R2, half * T), BF16), V((ring, T, R2), BF16), V((2, R2, 128), F32),
        V((4, 2 * UR, D), BF16), V((4, 2 * UR, D), BF16),
        V((2, R, F), F32), V((R, F), F32),
        V((max(1, cols - 1), 2, QR, F), F32), V((max(1, cols - 1), QR, F), F32),
        V((2, R, F), BF16), V((2, R2, D), BF16), V((2, T, D), F32),
        V((2, T // 2, D), BF16), V((half, T, D), BF16), V((half, T, D), BF16),
        V((2, 2 * UR, D), BF16), V((2, R2, F), BF16),
        V((max(1, groups - 1), 2, 2 * F, share), BF16), V((max(1, groups - 1), 2, 2 * F, share), BF16),
        DMA((2,)), DMA((4,)), DMA((4,)),
        DMA((2, half)), DMA((2, half)),
        DMA((2, 2, half, 2)), DMA((2, 2, half, 2)),
        DMA((cols,)), DMA((cols,)), DMA((cols,)), DMA((cols,)), DMA((cols,)), DMA((cols,)),
        DMA((2, half, 2)), DMA((2, half, 2)),
        DMA((groups,)), DMA((groups,)),
        pltpu.SemaphoreType.REGULAR,
    ]
    vmem = pl.BlockSpec(memory_space=pltpu.VMEM)
    grad_tokens, grad_in = pl.pallas_call(
        functools.partial(kernel, cap, ring, cols, groups, stagger),
        out_shape=(jax.ShapeDtypeStruct((T, D), BF16), jax.ShapeDtypeStruct((2, 2 * F, share), F32)),
        in_specs=[vmem, vmem, vmem, vmem, pl.BlockSpec(memory_space=pl.ANY), pl.BlockSpec(memory_space=pl.ANY)],
        out_specs=(vmem, vmem),
        scratch_shapes=scratch,
        compiler_params=pltpu.CompilerParams(
            collective_id=0, has_side_effects=True, vmem_limit_bytes=56 * 1024 * 1024
        ),
        cost_estimate=pl.CostEstimate(flops=10**10, bytes_accessed=10**7, transcendentals=10**5),
    )(expert_ids.T, gate_codes.T, tokens, cotangent, jnp.swapaxes(w_in, 1, 2), w_out)
    return grad_tokens, jnp.swapaxes(grad_in, 1, 2)


def solution(mesh):
    placed = (
        P(("expert", "dp"), "col"),
        P(("expert", "dp"), "col"),
        P(("expert", "dp"), None),
        P(("expert", "dp"), None),
        P("expert", "col", None),
        P("expert", None, "col"),
    )
    return jax.shard_map(
        functools.partial(per_device, STAGGER),
        mesh=mesh,
        in_specs=placed,
        out_specs=(P(("expert", "dp"), "col"), P("expert", ("col", "dp"), None)),
        check_vma=False,
    )


STAGGER = False
```

time: 456 us -> 202 us (0.44)
  waiting for transfers between devices: 344 us -> 0 us
  Pallas kernels: 0 us -> 197 us
  starting transfers between devices: 37.7 us -> 0 us
  local copies, waits for them, and re-layouts: 37.6 us -> 3.83 us
  between operations: 14.3 us -> 0.64 us
  other arithmetic: 12.4 us -> 0 us
  matrix products: 7.39 us -> 0 us
    all_to_all x3 -> x0, waiting for transfers between devices: 256 us -> none  [the longest x2 189 us: send_rows(): lax.all_to_all(block, 'expert', split_axis=0, concat_axis=1, tiled=True)]
    pallas_call x0 -> x1, Pallas kernels: none -> 197 us  [per_device(): pl.pallas_call(functools.partial(kernel, cap, ring, cols, groups, stagger...]
    psum x1 -> x0, waiting for transfers between devices: 88.4 us -> none  [per_device(): gate_up, hidden_grad = lax.psum((gate_part, hidden_part), 'col')]
    all_to_all x3 -> x0, starting transfers between devices: 37.5 us -> none  [the longest x2 24.2 us: send_rows(): lax.all_to_all(block, 'expert', split_axis=0, concat_axis=1, tiled=True)]
    gather x5 -> x0, local copies, waits for them, and re-layouts: 14.3 us -> none  [the longest x2 4.38 us: per_device(): tokens[token_of_slot]]
    all_to_all x3 -> x0, local copies, waits for them, and re-layouts: 9.04 us -> none  [the longest x2 7.14 us: send_rows(): lax.all_to_all(block, 'expert', split_axis=0, concat_axis=1, tiled=True)]
    dot_general x4 -> x0, matrix products: 7.39 us -> none  [the longest x1 3.15 us: per_device(): jnp.einsum('erd,erf->edf', rows_in, grad_gate_up, preferred_element_type=...]
  transfers between devices with their start and end apart: 5 -> 0, of which waited for: 4 -> 0; matrix products, arithmetic and copies ran while one was open for 6% -> 0% of each run, Pallas kernels for 0% -> 0%
where the time goes in v1:
time: 202 us
  Pallas kernels  197 us (98%)
  local copies, waits for them, and re-layouts  3.83 us (2%)
    pallas_call x1, Pallas kernels, per_device(): pl.pallas_call(functools.partial(kernel, cap, ring, cols, groups, stagger...  197 us

profile of v1, /device:TPU:6, one launch (start us, length us, event | category | flops | bytes accessed | tf_op | source)
XLA Modules:
  0.0 201.5 jit_solution(6210083826936025823)
XLA Ops:
  0.6 197.1 %shard_map.77 = (bf16[128,1024]{1,0:T(8,128)(2,1)}, f32[2,448,256]{2,1,0:T(8,128)}) custom-call(s32[4,128]{1,0:T(4,128)} %bitcast.6, s32[4,128]{1,0:T(4,128)} %bitcast.7, bf16[128,1024]{1,0:T(8,128)(2,1)} %tok_ref.1, bf16[128,1024]{1,0:T(8,128)(2,1)} %cot_ref.1, bf16[2,448,1024]{2,1,0:T(8,128)(2,1)} %bitcast.5, bf16[2,224,1024]{2,1,0:T(8,128)(2,1)} %wout_ref.1), custom_call_target="tpu_custom_call" | custom-call | flops 10000000000 | bytes 10000000 | tf_op jit(solution)/shard_map/pallas_call | solution.py:402
  197.7 1.7 copy.10
  199.4 2.2 %copy.11 = f32[2,256,448]{1,2,0:T(8,128)} copy(f32[2,256,448]{1,2,0:T(8,128)} %bitcast.4) | data formatting | bytes 1835008

commit v2 on v1

v2 whole, which is shorter than its diff:
```python
import functools

import jax
import jax.numpy as jnp
from jax import lax
from jax.experimental import pallas as pl
from jax.experimental.pallas import tpu as pltpu
from jax.sharding import PartitionSpec as P

MESH = pl.DeviceIdType.MESH
BF16, F32 = jnp.bfloat16, jnp.float32
TILE = 256


def dot(a, b):
    return jnp.dot(a, b, preferred_element_type=F32)


def dot_nt(a, b):
    return lax.dot_general(a, b, (((1,), (1,)), ((), ())), preferred_element_type=F32)


def dot_tn(a, b):
    return lax.dot_general(a, b, (((0,), (0,)), ((), ())), preferred_element_type=F32)


def kernel(
    cap, ring, cols, groups, plan,
    ids_ref, codes_ref, tok_ref, cot_ref, win_ref, wout_ref,
    gtok_ref, gin_ref,
    aux, land_t, land_c, win4, wout4, pick, pick_t, slot_w, xt, xc,
    part_gu, part_h, recv_gu, recv_h, sa, hh, gg, rg, contrib, rs_f, rs_r, rs_l,
    peer_x, peer_g, dp_out, dp_in,
    s_loc, s_peer, r_peer, s_aux, r_aux, s_ag, r_ag, s_gu, r_gu, s_h, r_h, s_sa, r_sa, s_hh, r_hh, s_rs, r_rs, s_dp, r_dp, go,
):
    T, D = tok_ref.shape
    F = wout_ref.shape[1]
    half = ring // 2
    NB = half
    UR = cap * NB
    R2 = 4 * UR
    R = 2 * R2
    QR = R // cols
    CH = plan["gather_chunks"]
    TC = T // CH
    RC = plan["return_chunks"]
    TR = T // RC
    lead = plan["lead"]
    tile = min(TILE, D)
    me = lax.axis_index("expert")
    z, core = me // 2, me % 2
    my_q = lax.axis_index("col")
    my_g = lax.axis_index("dp")
    right = {"expert": lax.rem(me + 2, 2 * ring)}
    left = {"expert": lax.rem(me + 2 * ring - 2, 2 * ring)}
    mate = {"expert": me + 1 - 2 * core}
    cols_at = [{"col": lax.rem(my_q + d, cols)} for d in range(cols)]
    groups_at = [{"dp": lax.rem(my_g + d, groups)} for d in range(groups)]
    ways = (right, left)

    partners = [right, left, mate] + cols_at[1:] + groups_at[1:]
    barrier = pltpu.get_barrier_semaphore()
    for other in partners:
        pl.semaphore_signal(barrier, inc=1, device_id=other, device_id_type=MESH)
    pl.semaphore_wait(barrier, len(partners))

    sent = []

    def ready(src, dst, send_sem, recv_sem, where):
        copy = pltpu.make_async_remote_copy(
            src_ref=src, dst_ref=dst, send_sem=send_sem, recv_sem=recv_sem, device_id=where, device_id_type=MESH
        )
        sent.append(copy)
        return copy

    def push(*copy):
        copy = ready(*copy)
        copy.start()
        return copy

    mine = pl.ds(2 * core, 2)
    local = [
        pltpu.make_async_copy(win_ref, win4.at[mine], s_loc.at[0]),
        pltpu.make_async_copy(wout_ref, wout4.at[mine], s_loc.at[1]),
    ]
    for copy in local:
        copy.start()
    w_in_copy = push(win_ref, win4.at[mine], s_peer.at[0], r_peer.at[0], mate)
    w_out_copy = push(wout_ref, wout4.at[mine], s_peer.at[1], r_peer.at[1], mate)

    codes = codes_ref[...].astype(F32)
    aux[0, 0:4, :] = ids_ref[...].astype(F32)
    aux[0, 4:8, :] = codes / jnp.sum(codes, axis=0, keepdims=True)
    land_t[0:T, :] = tok_ref[...]
    land_c[0:T, :] = cot_ref[...]

    if lead:
        @pl.when(core == 1)
        def _():
            pl.semaphore_wait(go.at[0], 1)

    def place(way, k):
        if k == 0:
            return 0
        if k == half:
            return 2 * half - 1
        return 2 * k if way == 0 else 2 * k - 1

    land = (land_t, land_c)
    ag = {}
    aux_copy = {}

    def carries(way, k, c):
        return k < half or c // (CH // 2) == way

    def pass_on(arr, way, k, c):
        if k > half or not carries(way, k, c):
            return
        src = land[arr].at[pl.ds(place(way, k - 1) * T + c * TC, TC)]
        dst = land[arr].at[pl.ds(place(way, k) * T + c * TC, TC)]
        ag[arr, way, k, c] = push(src, dst, s_ag.at[arr, way, k - 1, c], r_ag.at[arr, way, k - 1, c], ways[way])

    def pass_aux(way, k):
        if k < half or (k == half and way == 0):
            aux_copy[way, k] = push(
                aux.at[place(way, k - 1)], aux.at[place(way, k)],
                s_aux.at[way, k - 1], r_aux.at[way, k - 1], ways[way],
            )

    def arrived(arr, k):
        if lead:
            for turn, at in enumerate((lead, plan["release"])):
                if (arr, k) == at:
                    pl.semaphore_signal(go.at[turn], inc=1, device_id=mate, device_id_type=MESH)
        for c in range(CH):
            for way in range(2):
                if (arr, way, k, c) in ag:
                    ag[arr, way, k, c].wait_recv()
                    pass_on(arr, way, k + 1, c)
            if c == 0 and arr == 0:
                for way in range(2):
                    if (way, k) in aux_copy:
                        aux_copy[way, k].wait_recv()
                        pass_aux(way, k + 1)
            if k < half:
                work(arr, k if c == CH - 1 else k - 1)

    before = (lax.broadcasted_iota(jnp.int32, (T, T), 0) < lax.broadcasted_iota(jnp.int32, (T, T), 1)).astype(F32).astype(BF16)
    block_of = lax.broadcasted_iota(jnp.int32, (NB, T), 0)

    def build_pick(h):
        info = aux[h * NB:(h + 1) * NB]
        ids = [info[:, k, :] for k in range(4)]
        weights = [info[:, 4 + k, :] for k in range(4)]
        member, weight = [], []
        for e in range(4):
            number = (4 * z + e).astype(F32)
            hits = [ids[k] == number for k in range(4)]
            member.append(sum(jnp.where(hit, 1.0, 0.0) for hit in hits))
            weight.append(sum(jnp.where(hits[k], weights[k], 0.0) for k in range(4)))
        order = dot(jnp.concatenate(member, axis=0).astype(BF16), before)
        chosen, rows_w = [], []
        for e in range(4):
            at = order[e * NB:(e + 1) * NB]
            for j in range(cap):
                one = jnp.where(at == float(j), member[e], 0.0)
                chosen.append(one)
                rows_w.append(jnp.sum(one * weight[e], axis=1, keepdims=True))
        slot_w[h] = jnp.broadcast_to(jnp.concatenate(rows_w, axis=0), (R2, 128))
        for i in range(NB):
            rows = jnp.concatenate([jnp.where(block_of == i, one, 0.0) for one in chosen], axis=0)
            pick[h, :, i * T:(i + 1) * T] = rows.astype(BF16)
            pick_t[(h * NB + i) * T:(h * NB + i + 1) * T, :] = rows.T.astype(BF16)

    def compact(arr, h, lo, hi):
        def body(n, carry):
            at = pl.ds(pl.multiple_of(n * tile, tile), tile)
            rows = dot(pick[h], land[arr][h * NB * T:(h + 1) * NB * T, at])
            if arr == 1:
                rows = rows * slot_w[h][:, 0:1]
            rows = rows.astype(BF16)
            for e in range(4):
                (xt, xc)[arr][e, h * UR:(h + 1) * UR, at] = rows[e * UR:(e + 1) * UR]
            return carry
        lax.fori_loop(lo * (D // tile) // 2, hi * (D // tile) // 2, body, 0)

    def rows_at(e, h):
        return pl.ds(pl.multiple_of(e * 2 * UR + h * UR, UR), UR)

    def gate_up(h, lo):
        def body(e, carry):
            x = xt[e, h * UR:(h + 1) * UR, :]
            part_gu[0, rows_at(e, h), :] = dot_nt(x, win4[e, 0:F, :])
            part_gu[1, rows_at(e, h), :] = dot_nt(x, win4[e, F:2 * F, :])
            return carry
        lax.fori_loop(lo, lo + 2, body, 0)

    def hidden(h):
        def body(e, carry):
            part_h[rows_at(e, h), :] = dot_nt(xc[e, h * UR:(h + 1) * UR, :], wout4[e]).astype(BF16)
            return carry
        lax.fori_loop(0, 4, body, 0)

    split = QR == UR

    def rows_of(d):
        return pl.ds(pl.multiple_of(lax.rem(my_q + d, cols) * QR, QR), QR)

    def in_half(d, h):
        return lax.rem(lax.rem(my_q + d, cols), 2) == h

    def when_half(d, h, fn):
        if split:
            pl.when(in_half(d, h))(fn)
        elif h == 1:
            fn()

    far_first = sorted(range(1, cols), key=lambda d: -min(d, cols - d))
    peer_copies = []
    gu_copies = {d: ready(part_gu.at[:, rows_of(d)], recv_gu.at[d - 1], s_gu.at[d - 1], r_gu.at[d - 1], cols_at[d]) for d in far_first}
    h_copies = {d: ready(part_h.at[rows_of(d)], recv_h.at[d - 1], s_h.at[d - 1], r_h.at[d - 1], cols_at[d]) for d in far_first}
    hh_copies = {d: ready(hh.at[rows_of(0)], hh.at[rows_of(0)], s_hh.at[d - 1], r_hh.at[d - 1], cols_at[d]) for d in far_first}
    sa_copies = {d: ready(sa.at[:, rows_of(0)], sa.at[:, rows_of(0)], s_sa.at[d - 1], r_sa.at[d - 1], cols_at[d]) for d in far_first}

    def weights_ready():
        for copy in local:
            copy.wait()
        w_in_copy.wait_recv()
        w_out_copy.wait_recv()

    def send_gate_up(h):
        for d in far_first:
            when_half(d, h, gu_copies[d].start)
        if h == 1:
            peer_copies.append(push(xt.at[pl.ds(2 - 2 * core, 2)], peer_x, s_peer.at[2], r_peer.at[2], mate))

    def send_hidden(h):
        for d in far_first:
            when_half(d, h, h_copies[d].start)

    def share_slopes():
        own = rows_of(0)
        gate, up = part_gu[0, own, :], part_gu[1, own, :]
        for d in range(1, cols):
            gu_copies[d].wait_recv()
        for d in range(cols - 1):
            gate = gate + recv_gu[d, 0]
            up = up + recv_gu[d, 1]
        s = jax.nn.sigmoid(gate)
        sa[0, own, :] = (up * s * (1.0 + gate * (1.0 - s))).astype(BF16)
        sa[1, own, :] = (gate * s).astype(BF16)
        for d in far_first:
            sa_copies[d].start()

    def share_hidden():
        own = rows_of(0)
        grad = part_h[own, :].astype(F32)
        for d in range(1, cols):
            h_copies[d].wait_recv()
        for d in range(cols - 1):
            grad = grad + recv_h[d].astype(F32)
        hh[own, :] = grad.astype(BF16)
        for d in far_first:
            hh_copies[d].start()

    def landing(ref, sems, d):
        where = ref.at[rows_of(cols - d)] if len(ref.shape) == 2 else ref.at[:, rows_of(cols - d)]
        return pltpu.make_async_remote_copy(
            src_ref=where, dst_ref=where, send_sem=sems[0].at[d - 1], recv_sem=sems[1].at[d - 1],
            device_id=cols_at[d], device_id_type=MESH,
        )

    def slopes_here():
        for d in range(1, cols):
            landing(sa, (s_sa, r_sa), d).wait_recv()

    def hidden_here(h):
        for d in range(1, cols):
            when_half(cols - d, h, landing(hh, (s_hh, r_hh), d).wait_recv)

    tasks = [
        (0, half // 2, lambda: build_pick(0)),
        (0, half // 2 + 1, lambda: compact(0, 0, 0, 1)),
        (0, half // 2 + 1, lambda: compact(0, 0, 1, 2)),
        (0, half // 2 + 1, weights_ready),
        (0, half // 2 + 1, lambda: gate_up(0, 0)),
        (0, half // 2 + 1, lambda: gate_up(0, 2)),
        (0, half // 2 + 1, lambda: send_gate_up(0)),
        (1, 1, lambda: build_pick(1)),
        (1, 1, lambda: compact(0, 1, 0, 1)),
        (1, 1, lambda: compact(0, 1, 1, 2)),
        (1, 1, lambda: gate_up(1, 0)),
        (1, 1, lambda: gate_up(1, 2)),
        (1, 1, lambda: send_gate_up(1)),
        (1, half // 2, lambda: compact(1, 0, 0, 1)),
        (1, half // 2, lambda: compact(1, 0, 1, 2)),
        (1, half // 2, lambda: hidden(0)),
        (1, half // 2, lambda: send_hidden(0)),
        (1, half - 2, share_slopes),
    ]
    if split:
        tasks.append((1, half - 1, lambda: pl.when(in_half(0, 0))(share_hidden)))

    def work(arr, k):
        if tasks and (tasks[0][0], tasks[0][1]) <= (arr, k):
            tasks.pop(0)[2]()

    for way in range(2):
        pass_aux(way, 1)
    for arr in range(2):
        for c in range(CH):
            for way in range(2):
                pass_on(arr, way, 1, c)
        if arr == 1:
            arrived(0, half)
        for k in range(1, half):
            arrived(arr, k)
    while tasks:
        work(2, 0)
    arrived(1, half)
    compact(1, 1, 0, 2)
    hidden(1)
    send_hidden(1)
    slopes_here()

    def route_grad(h):
        def body(e, carry):
            rows = rows_at(e, h)
            grad = hh[rows, :].astype(F32)
            g0 = (grad * sa[0, rows, :].astype(F32)).astype(BF16)
            g1 = (grad * sa[1, rows, :].astype(F32)).astype(BF16)
            gg[0, rows, :] = g0
            gg[1, rows, :] = g1
            at = pl.ds(pl.multiple_of(e * UR, UR), UR)
            rg[h, at, :] = (dot(g0, win4[e, 0:F, :]) + dot(g1, win4[e, F:2 * F, :])).astype(BF16)
            return carry
        lax.fori_loop(0, 4, body, 0)

    if split:
        hidden_here(0)
        route_grad(0)
        pl.when(in_half(0, 1))(share_hidden)
        hidden_here(1)
    else:
        share_hidden()
        hidden_here(1)
        route_grad(0)
    route_grad(1)
    theirs = pl.ds(pl.multiple_of((1 - core) * R2, R2), R2)
    peer_copies.append(push(gg.at[:, theirs], peer_g, s_peer.at[3], r_peer.at[3], mate))

    def contributions(h):
        rows = slice(h * NB * T, (h + 1) * NB * T)

        def body(n, carry):
            lanes = pl.ds(pl.multiple_of(n * tile, tile), tile)
            contrib[rows, lanes] = dot(pick_t[rows], rg[h, :, lanes])
            return carry
        lax.fori_loop(0, D // tile, body, 0)

    share = D // groups

    def weight_grad(d):
        lanes = pl.ds(pl.multiple_of(lax.rem(my_g + d, groups) * share, share), share)
        for l in range(2):
            rows = pl.ds(pl.multiple_of((2 * core + l) * 2 * UR, 2 * UR), 2 * UR)
            x = jnp.concatenate([xt[2 * core + l, :, lanes], peer_x[l, :, lanes]], axis=0)
            for g in range(2):
                grads = jnp.concatenate([gg[g, rows, :], peer_g[g, l * 2 * UR:(l + 1) * 2 * UR, :]], axis=0)
                value = dot_tn(grads, x)
                if d == 0:
                    gin_ref[l, g * F:(g + 1) * F, :] = value
                else:
                    dp_out[d - 1, l, g * F:(g + 1) * F, :] = value.astype(BF16)

    dp_copies = []

    def send_weight_grad(d):
        weight_grad(d)
        dp_copies.append(push(dp_out.at[d - 1], dp_in.at[d - 1], s_dp.at[d - 1], r_dp.at[d - 1], groups_at[d]))

    def peers_ready():
        for copy in peer_copies:
            copy.wait_recv()

    later = [lambda: contributions(0), peers_ready]
    for d in sorted(range(1, groups), key=lambda d: -min(d, groups - d)):
        later.append(functools.partial(send_weight_grad, d))
    later.append(lambda: weight_grad(0))

    contributions(1)
    if lead:
        pl.semaphore_wait(go.at[1], 1)

        @pl.when(core == 0)
        def _():
            pl.semaphore_wait(go.at[0], 1)
    rs = (rs_r, rs_l)
    rs_copy = {}

    def rs_send(way, k, c, src):
        rs_copy[way, k, c] = push(
            src, rs[way].at[k - 1, pl.ds(c * TR, TR)], s_rs.at[way, k - 1, c], r_rs.at[way, k - 1, c], ways[way]
        )

    for c in range(RC // 2):
        for way in range(2):
            cc = c + way * (RC // 2)
            at = (2 * half - 1) * T + cc * TR
            rs_f[cc * TR:(cc + 1) * TR, :] = contrib[at:at + TR, :].astype(BF16)
            rs_send(way, 1, cc, rs_f.at[pl.ds(cc * TR, TR)])
    if half < 4:
        later.pop(0)()
    for k in range(2, half + 1):
        o = half + 1 - k
        for c in range(RC):
            for way in range(2):
                at = (2 * o - 1 + way) * T + c * TR
                total = contrib[at:at + TR, :]
                if (way, k - 1, c) in rs_copy:
                    rs_copy[way, k - 1, c].wait_recv()
                    total = total + rs[way][k - 2, c * TR:(c + 1) * TR, :].astype(F32)
                rs[way][k - 2, c * TR:(c + 1) * TR, :] = total.astype(BF16)
                rs_send(way, k, c, rs[way].at[k - 2, pl.ds(c * TR, TR)])
        if later:
            later.pop(0)()
    while later:
        later.pop(0)()
    for c in range(RC):
        at = slice(c * TR, (c + 1) * TR)
        total = contrib[at, :]
        for way in range(2):
            rs_copy[way, half, c].wait_recv()
            total = total + rs[way][half - 1, at, :].astype(F32)
        gtok_ref[at, :] = total.astype(BF16)
    for copy in dp_copies:
        copy.wait_recv()
    for l in range(2):
        total = gin_ref[l]
        for d in range(groups - 1):
            total = total + dp_in[d, l].astype(F32)
        gin_ref[l] = total
    for copy in sent:
        copy.wait_send()


def per_device(plan, tokens, cotangent, expert_ids, gate_codes, w_in, w_out):
    T, D = tokens.shape
    top = expert_ids.shape[1]
    F = w_out.shape[1]
    owners, cols, groups = lax.axis_size("expert"), lax.axis_size("col"), lax.axis_size("dp")
    ring = owners // 2
    half = ring // 2
    experts = w_in.shape[0] * owners
    cap = T * top // experts * 5 // 4
    UR = cap * half
    R2, R = 4 * UR, 8 * UR
    QR = R // cols
    share = D // groups
    rc, gc = plan["return_chunks"], plan["gather_chunks"]
    V = pltpu.VMEM
    DMA = pltpu.SemaphoreType.DMA
    scratch = [
        V((ring, 8, T), F32),
        V((ring * T, D), BF16), V((ring * T, D), BF16),
        V((4, 2 * F, D), BF16), V((4, F, D), BF16),
        V((2, R2, half * T), BF16), V((ring * T, R2), BF16), V((2, R2, 128), F32),
        V((4, 2 * UR, D), BF16), V((4, 2 * UR, D), BF16),
        V((2, R, F), F32), V((R, F), BF16),
        V((max(1, cols - 1), 2, QR, F), F32), V((max(1, cols - 1), QR, F), BF16),
        V((2, R, F), BF16), V((R, F), BF16), V((2, R, F), BF16), V((2, R2, D), BF16), V((ring * T, D), F32),
        V((T, D), BF16), V((half, T, D), BF16), V((half, T, D), BF16),
        V((2, 2 * UR, D), BF16), V((2, R2, F), BF16),
        V((max(1, groups - 1), 2, 2 * F, share), BF16), V((max(1, groups - 1), 2, 2 * F, share), BF16),
        DMA((2,)), DMA((4,)), DMA((4,)),
        DMA((2, half)), DMA((2, half)),
        DMA((2, 2, half, gc)), DMA((2, 2, half, gc)),
        *[DMA((cols,))] * 8,
        DMA((2, half, rc)), DMA((2, half, rc)),
        DMA((groups,)), DMA((groups,)),
        pltpu.SemaphoreType.REGULAR((2,)),
    ]
    vmem = pl.BlockSpec(memory_space=pltpu.VMEM)
    grad_tokens, grad_in = pl.pallas_call(
        functools.partial(kernel, cap, ring, cols, groups, plan),
        out_shape=(jax.ShapeDtypeStruct((T, D), BF16), jax.ShapeDtypeStruct((2, 2 * F, share), F32)),
        in_specs=[vmem, vmem, vmem, vmem, pl.BlockSpec(memory_space=pl.ANY), pl.BlockSpec(memory_space=pl.ANY)],
        out_specs=(vmem, vmem),
        scratch_shapes=scratch,
        compiler_params=pltpu.CompilerParams(
            collective_id=0, has_side_effects=True, vmem_limit_bytes=56 * 1024 * 1024
        ),
        cost_estimate=pl.CostEstimate(flops=10**10, bytes_accessed=10**7, transcendentals=10**5),
    )(expert_ids.T, gate_codes.T, tokens, cotangent, jnp.swapaxes(w_in, 1, 2), w_out)
    return grad_tokens, jnp.swapaxes(grad_in, 1, 2)


def solution(mesh):
    placed = (
        P(("expert", "dp"), "col"),
        P(("expert", "dp"), "col"),
        P(("expert", "dp"), None),
        P(("expert", "dp"), None),
        P("expert", "col", None),
        P("expert", None, "col"),
    )
    return jax.shard_map(
        functools.partial(per_device, PLAN),
        mesh=mesh,
        in_specs=placed,
        out_specs=(P(("expert", "dp"), "col"), P("expert", ("col", "dp"), None)),
        check_vma=False,
    )


PLAN = {"lead": None, "release": (1, 6), "gather_chunks": 4, "return_chunks": 4}
```

time: 202 us -> 189 us (0.936)
  Pallas kernels: 197 us -> 185 us
    pallas_call x1, Pallas kernels: 197 us -> 185 us  [per_device(): pl.pallas_call(functools.partial(kernel, cap, ring, cols, groups, plan),...]
where the time goes in v2:
time: 189 us
  Pallas kernels  185 us (98%)
  local copies, waits for them, and re-layouts  3.83 us (2%)
    pallas_call x1, Pallas kernels, per_device(): pl.pallas_call(functools.partial(kernel, cap, ring, cols, groups, plan),...  185 us
    unnamed x2, local copies, waits for them, and re-layouts  3.83 us

profile of v2, /device:TPU:6, one launch (start us, length us, event | category | flops | bytes accessed | tf_op | source)
XLA Modules:
  0.0 189.2 jit_solution(12884730120758099639)
XLA Ops:
  0.6 184.8 %shard_map.77 = (bf16[128,1024]{1,0:T(8,128)(2,1)}, f32[2,448,256]{2,1,0:T(8,128)}) custom-call(s32[4,128]{1,0:T(4,128)} %bitcast.6, s32[4,128]{1,0:T(4,128)} %bitcast.7, bf16[128,1024]{1,0:T(8,128)(2,1)} %tok_ref.1, bf16[128,1024]{1,0:T(8,128)(2,1)} %cot_ref.1, bf16[2,448,1024]{2,1,0:T(8,128)(2,1)} %bitcast.5, bf16[2,224,1024]{2,1,0:T(8,128)(2,1)} %wout_ref.1), custom_call_target="tpu_custom_call" | custom-call | flops 10000000000 | bytes 10000000 | tf_op jit(solution)/shard_map/pallas_call | solution.py:484
  185.4 1.7 copy.10
  187.1 2.2 %copy.11 = f32[2,256,448]{1,2,0:T(8,128)} copy(f32[2,256,448]{1,2,0:T(8,128)} %bitcast.4) | data formatting | bytes 1835008
